TPU v7x, 32 devices: a whole 2x2x4 slice. The times are simulated.
32 devices in a mesh: groups: 2 (over x), row: 4 (over y, core), col: 4 (over z).
Axes of the slice: x: 2, y: 2, z: 4, core: 2. Of those that a mesh axis runs over, the one named last changes fastest.
Arguments:
- embeddings: float32 [32, 8192], P(None, ('groups', 'row', 'col')), parts along dimension 1, may hold values from -6 to 6
- inv_length: float32 [32], replicated, may hold values from 0.25 to 0.6
- task_cov: float32 [16, 16], replicated, may hold values from -0.1 to 2.4, as said below
- noise: float32 [16], replicated, may hold values from 0.2 to 1
- targets: float32 [16, 8192], P(None, ('groups', 'row', 'col')), parts along dimension 1, may hold values from -25 to 25
Outputs:
- solution_field: float32 [16, 8192], P(None, ('groups', 'row', 'col')), parts along dimension 1
- residual: float32 [16, 8192], P(None, ('groups', 'row', 'col')), parts along dimension 1
There are 2 independent parts, one for each index of `groups`. A program takes and returns all parts, laid end to end along the dimension named above; an argument that names none is the same for every part. Nothing has to cross between parts.
Inputs may be any that keep to these rules, and one draw needn't show every extreme that they name: `task_cov`: symmetric; each diagonal entry exceeds the sum of the magnitudes of the other entries of its row.
All inputs are finite; a program needn't handle non-finite values.
Results may differ from a plain program's by a relative error of at most 0.0003.
Values sent between devices are 32-bit elements; how exact they have to be, the bound alone decides.
A program may use at most 128 MiB of HBM per device.

v0:
```python
import jax
import jax.numpy as jnp
from jax import lax
from jax.sharding import PartitionSpec as P

ITERS = 2


def squares(residual):
    return lax.psum(jnp.sum(residual * residual), ("row", "col"))


def on_device(embeddings, inv_length, task_cov, noise, targets):
    scaled = embeddings * inv_length[:, None]
    cols_emb = lax.all_gather(scaled, ("row", "col"), axis=1, tiled=True)
    rows_sq = jnp.sum(scaled * scaled, axis=0)
    cols_sq = jnp.sum(cols_emb * cols_emb, axis=0)
    solution_field = jnp.zeros_like(targets)
    residual = targets
    direction = targets
    norm_now = squares(residual)
    for step in range(ITERS):
        cross = jnp.einsum("kc,kr->cr", cols_emb, scaled, precision=lax.Precision.HIGHEST)
        tile = jnp.exp(-0.5 * (cols_sq[:, None] + rows_sq[None, :] - 2.0 * cross))
        coupled = jnp.dot(
            lax.all_gather(direction, ("row", "col"), axis=1, tiled=True),
            tile,
            precision=lax.Precision.HIGHEST,
        )
        image = (
            jnp.dot(task_cov, coupled, precision=lax.Precision.HIGHEST) + noise[:, None] * direction
        )
        alpha = norm_now / lax.psum(jnp.sum(direction * image), ("row", "col"))
        solution_field = solution_field + alpha * direction
        residual = residual - alpha * image
        if step + 1 < ITERS:
            norm_next = squares(residual)
            direction = residual + norm_next / norm_now * direction
            norm_now = norm_next
    return (solution_field, residual)


def solution(mesh):
    return jax.shard_map(
        on_device,
        mesh=mesh,
        in_specs=(
            P(None, ("groups", "row", "col")),
            P(),
            P(),
            P(),
            P(None, ("groups", "row", "col")),
        ),
        out_specs=(P(None, ("groups", "row", "col")), P(None, ("groups", "row", "col"))),
        check_vma=False,
    )
```

profile of v0, /device:TPU:0, one launch (start us, length us, event | category | flops | bytes accessed | tf_op | source)
XLA Modules:
  0.0 219.5 jit_solution(4017332272513371984)
XLA Ops:
  0.6 0.0 copy-start
  0.6 0.0 copy-start.2
  0.7 0.9 multiply_reduce_fusion.1
  1.5 38.7 %all_gather.9 = f32[32,4096]{1,0:T(8,128)S(1)} all-gather(f32[32,256]{1,0:T(8,128)S(1)} %get-tuple-element.7), channel_id=1, replica_groups=mesh['groups'=2,'row'=4,'col'=4] {'row','col'}, dimensions={1}, use_global_device_ids=true | all-gather | bytes 557056 | tf_op jit(solution)/shard_map/all_gather | solution.py:15
  40.2 0.1 multiply_reduce_fusion
  40.3 0.0 copy-start.3
  40.3 4.8 %fusion.2 = f32[4096,256]{1,0:T(8,128)S(1)} fusion(f32[32,4096]{1,0:T(8,128)S(1)} %all_gather.9, f32[32,256]{1,0:T(8,128)S(1)} %get-tuple-element.7, f32[256]{0:T(256)S(1)} %get-tuple-element.6, f32[4096]{0:T(1024)S(1)} %multiply_reduce_fusion), kind=kOutput, calls=%fused_computation.3 | convolution fusion | flops 406847488 | bytes 4768768 | tf_op jit(solution)/shard_map/kc,kr->cr/dot_general | solution.py:23
  45.2 0.0 copy-done.2
  45.2 0.0 copy-start.1
  45.2 30.7 %all_gather.10 = f32[16,4096]{1,0:T(8,128)S(1)} all-gather(f32[16,256]{1,0:T(8,128)S(1)} %copy-done.2), channel_id=1, replica_groups=mesh['groups'=2,'row'=4,'col'=4] {'row','col'}, dimensions={1}, use_global_device_ids=true | all-gather | bytes 278528 | tf_op jit(solution)/shard_map/all_gather | solution.py:26
  75.9 0.0 copy-done.1
  75.9 6.7 %fusion.5 = f32[256,16]{1,0:T(8,128)S(1)} fusion(f32[4096,256]{1,0:T(8,128)S(1)} %fusion.2, f32[16,4096]{1,0:T(8,128)S(1)} %all_gather.10), kind=kOutput, calls=%fused_computation.19 | convolution fusion | flops 201326592 | bytes 4472832 | tf_op jit(solution)/shard_map/dot_general | solution.py:25
  82.5 0.0 copy-done
  82.5 0.0 copy-done.3
  82.5 0.8 multiply_reduce_fusion.4
  83.4 32.4 %all-reduce = (f32[]{:T(128)}, f32[]{:T(128)}) all-reduce(f32[]{:T(128)} %get-tuple-element.3, f32[]{:T(128)} %get-tuple-element.2), channel_id=1, replica_groups=mesh['groups'=2,'row'=4,'col'=4] {'row','col'}, use_global_device_ids=true, to_apply=%region_1.0 | all-reduce | flops 2 | bytes 16 | tf_op jit(solution)/shard_map/psum | solution.py:10
  117.1 0.6 multiply_reduce_fusion.3
  117.7 30.5 %psum.30 = f32[]{:T(128)} all-reduce(f32[]{:T(128)} %multiply_reduce_fusion.3), channel_id=1, replica_groups=mesh['groups'=2,'row'=4,'col'=4] {'row','col'}, use_global_device_ids=true, to_apply=%region_7.0 | all-reduce | flops 1 | bytes 8 | tf_op jit(solution)/shard_map/psum | solution.py:10
  149.5 32.8 %all_gather.11 = f32[16,4096]{1,0:T(8,128)S(1)} all-gather(f32[16,256]{1,0:T(8,128)S(1)} %multiply_add_fusion.1), channel_id=1, replica_groups=mesh['groups'=2,'row'=4,'col'=4] {'row','col'}, dimensions={1}, use_global_device_ids=true | all-gather | bytes 278528 | tf_op jit(solution)/shard_map/all_gather | solution.py:26
  182.3 3.9 %fusion.6 = f32[16,256]{1,0:T(8,128)S(1)} fusion(f32[16,4096]{1,0:T(8,128)S(1)} %all_gather.11, f32[4096,256]{1,0:T(8,128)} %copy-done.1), kind=kOutput, calls=%fused_computation.20 | convolution fusion | flops 201326592 | bytes 4472832 | tf_op jit(solution)/shard_map/dot_general | solution.py:25
  186.2 0.8 multiply_reduce_fusion.2
  187.0 30.5 %psum.31 = f32[]{:T(128)} all-reduce(f32[]{:T(128)} %get-tuple-element.11), channel_id=1, replica_groups=mesh['groups'=2,'row'=4,'col'=4] {'row','col'}, use_global_device_ids=true, to_apply=%region_9.0 | all-reduce | flops 1 | bytes 8 | tf_op jit(solution)/shard_map/psum | solution.py:33
  218.9 0.6 multiply_subtract_fusion
  (1 shorter events, 0.0 us)
Async XLA Ops:
  0.6 81.9 %copy-start = (f32[16,16]{1,0:T(8,128)S(1)}, f32[16,16]{1,0:T(8,128)}, u32[]{:S(2)}) copy-start(f32[16,16]{1,0:T(8,128)} %param.7) | copy-start | bytes 3076
  0.6 44.5 %copy-start.2 = (f32[16,256]{1,0:T(8,128)S(1)}, f32[16,256]{1,0:T(8,128)}, u32[]{:S(2)}) copy-start(f32[16,256]{1,0:T(8,128)} %param.9) | copy-start | bytes 49156
  40.3 42.2 %copy-start.3 = (f32[16]{0:T(128)S(1)}, f32[16]{0:T(128)}, u32[]{:S(2)}) copy-start(f32[16]{0:T(128)} %param.8) | copy-start | bytes 196
  45.2 30.7 %copy-start.1 = (f32[4096,256]{1,0:T(8,128)}, f32[4096,256]{1,0:T(8,128)S(1)}, u32[]{:S(2)}) copy-start(f32[4096,256]{1,0:T(8,128)S(1)} %fusion.2) | copy-start | bytes 12582916
where the time goes:
time: 220 us; the launch traced here: 219 us
  blocking collectives  196 us (89%)
  matrix products  17 us (8%)
  between operations  4.73 us (2%)
    all_gather x2, blocking collectives, on_device(): lax.all_gather(direction, ('row', 'col'), axis=1, tiled=True)  63.5 us
    psum x2, blocking collectives, squares(): return lax.psum(jnp.sum(residual * residual), ('row', 'col'))  62.8 us
    all_gather x1, blocking collectives, on_device(): cols_emb = lax.all_gather(scaled, ('row', 'col'), axis=1, tiled=True)  38.7 us
    psum x1, blocking collectives, on_device(): alpha = norm_now / lax.psum(jnp.sum(direction * image), ('row', 'col'))  30.5 us
    dot_general x2, matrix products, on_device(): jnp.dot(lax.all_gather(direction, ('row', 'col'), axis=1, tiled=True), ti...  10.6 us
    dot_general x1, matrix products, on_device(): jnp.einsum('kc,kr->cr', cols_emb, scaled, precision=lax.Precision.HIGHEST)  4.82 us

commit v1 on v0

v1 whole, which is shorter than its diff:
```python
import functools
import math

import jax
import jax.numpy as jnp
from jax import lax
from jax.experimental import pallas as pl
from jax.experimental.pallas import tpu as pltpu
from jax.sharding import PartitionSpec as P

MESH = pl.DeviceIdType.MESH
F32 = jnp.float32
BF16 = jnp.bfloat16
ROOT_LOG2E = math.sqrt(1.0 / math.log(2.0))


def partner(me, k, n):
    if n & (n - 1):
        return [(me + k) % n, (me + n - k) % n][: 1 if 2 * k == n else 2]
    other = me
    bit = 1
    while bit <= k:
        if k & bit:
            other = other + bit * (1 - 2 * ((me // bit) % 2))
        bit *= 2
    return [other]


def three_parts(x):
    high = x.astype(BF16)
    rest = x - high.astype(F32)
    mid = rest.astype(BF16)
    low = (rest - mid.astype(F32)).astype(BF16)
    return high, mid, low


def two_parts(x):
    high = x.astype(BF16)
    return jnp.concatenate([high, (x - high.astype(F32)).astype(BF16)], axis=0)


def kernel(nr, nc, e_hbm, len_hbm, cov_hbm, noise_hbm, t_hbm, sol_ref, res_ref,
           len_v, cov_v, noise_v, e_row, e_col, t_row, cov_b, left, right, k_high, k_low, v_row,
           part_out, part_in, cu_row, mix_out, mix_in, scal,
           sem_local, s_er, r_er, s_ec, r_ec, s_t, r_t, s_p, r_p, s_c, r_c, s_m, r_m, s_s, r_s):
    emb, width = e_hbm.shape
    tasks = t_hbm.shape[0]
    row, col = lax.axis_index("row"), lax.axis_index("col")
    rows_to = [partner(row, k, nr) for k in range(nr)]
    cols_to = [partner(col, k, nc) for k in range(nc)]

    barrier = pltpu.get_barrier_semaphore()
    for k in range(1, nc):
        for peer in cols_to[k]:
            pl.semaphore_signal(barrier, inc=1, device_id={"col": peer}, device_id_type=MESH)
    for k in range(1, nr):
        for peer in rows_to[k]:
            pl.semaphore_signal(barrier, inc=1, device_id={"row": peer}, device_id_type=MESH)
    count = sum(len(p) for p in cols_to[1:] + rows_to[1:])

    local = [
        pltpu.make_async_copy(src, dst, sem_local.at[i])
        for i, (src, dst) in enumerate(
            [(e_hbm, e_row.at[0]), (t_hbm, t_row.at[0]), (len_hbm, len_v), (cov_hbm, cov_v), (noise_hbm, noise_v)]
        )
    ]
    for copy in local:
        copy.start()
    pl.semaphore_wait(barrier, count)

    def to_col(src, dst, send, recv, k):
        return pltpu.make_async_remote_copy(
            src_ref=src, dst_ref=dst, send_sem=send.at[k], recv_sem=recv.at[k],
            device_id={"col": cols_to[k][0]}, device_id_type=MESH)

    def to_row(src, dst, send, recv, k):
        return pltpu.make_async_remote_copy(
            src_ref=src, dst_ref=dst, send_sem=send.at[k], recv_sem=recv.at[k],
            device_id={"row": rows_to[k][0]}, device_id_type=MESH)

    sent = []
    ec = {k: to_col(e_hbm, e_col.at[k], s_ec, r_ec, k) for k in range(1, nc)}
    er = {k: to_row(e_hbm, e_row.at[k], s_er, r_er, k) for k in range(1, nr)}
    tr = {k: to_row(t_hbm, t_row.at[k], s_t, r_t, k) for k in range(1, nr)}
    for group in (er, ec, tr):
        for k in group:
            group[k].start()
            sent.append(group[k])

    for copy in local:
        copy.wait()

    def as_column(x, n):
        eye = lax.broadcasted_iota(jnp.int32, (n, n), 0) == lax.broadcasted_iota(jnp.int32, (n, n), 1)
        return jnp.sum(jnp.where(eye, jnp.broadcast_to(x, (n, n)), 0.0), axis=1, keepdims=True)

    scale = as_column(len_v[...], emb) * ROOT_LOG2E
    noise = as_column(noise_v[...], tasks)
    for k in range(tasks):
        cov_b[k] = jnp.broadcast_to(cov_v[:, k : k + 1], (tasks, 128))

    def couple(x):
        halves = []
        for start in range(0, width, 128):
            acc = cov_b[0] * x[0:1, start : start + 128]
            for k in range(1, tasks):
                acc = acc + cov_b[k] * x[k : k + 1, start : start + 128]
            halves.append(acc)
        return jnp.concatenate(halves, axis=1)

    line = lax.broadcasted_iota(jnp.int32, (16, width), 0)
    depth = left.shape[2]

    def features(x):
        scaled = x * scale
        half = -0.5 * jnp.sum(scaled * scaled, axis=0, keepdims=True)
        return three_parts(scaled), [p.astype(F32) for p in three_parts(half)]

    def extra(parts, first):
        rows = jnp.where((line >= 3 - first) & (line < 6 - first), 1.0, 0.0).astype(F32)
        for i, p in enumerate(parts):
            rows = jnp.where(line == first + i, jnp.broadcast_to(p, rows.shape), rows)
        return rows.astype(BF16)

    def fill(used):
        return [jnp.zeros((depth - used, width), BF16)] if depth > used else []

    def left_of(x):
        (h, m, l), q = features(x)
        return jnp.concatenate([h, h, m, m, h, l, extra(q, 0)] + fill(6 * emb + 16), axis=0).T

    def right_of(x):
        (h, m, l), q = features(x)
        return jnp.concatenate([h, m, h, m, l, h, extra(q, 3)] + fill(6 * emb + 16), axis=0)

    def tile(j, i):
        power = jnp.dot(left[i], right[j], preferred_element_type=F32)
        k = jnp.exp2(power)
        high = k.astype(BF16)
        low = (k - high.astype(F32)).astype(BF16)
        k_high[j, i] = high
        k_low[j, i] = low
        return high, low

    def over_rows(body, init):
        if nr <= 4:
            acc = init
            for i in range(nr):
                acc = body(i, acc)
            return acc
        return lax.fori_loop(0, nr, body, init)

    def fold(acc):
        return acc[:tasks] + acc[tasks:]

    def zero():
        return jnp.zeros((2 * tasks, width), F32)

    def apply(j):
        def body(i, acc):
            v = v_row[i]
            acc = acc + jnp.dot(v, k_high[j, i], preferred_element_type=F32)
            return acc + jnp.dot(v, k_low[j, i], preferred_element_type=F32)
        return fold(over_rows(body, zero()))

    def make_and_apply(j):
        def body(i, acc):
            high, low = tile(j, i)
            v = v_row[i]
            acc = acc + jnp.dot(v, high, preferred_element_type=F32)
            return acc + jnp.dot(v, low, preferred_element_type=F32)
        return fold(over_rows(body, zero()))

    right[0] = right_of(e_row[0])
    for i in range(nr):
        if i:
            er[i].wait_recv()
        left[i] = left_of(e_row[i])
        if nr <= 4:
            tile(0, i)
    if nr > 4:
        over_rows(lambda i, acc: (tile(0, i), acc)[1], 0)
    for i in range(nr):
        if i:
            tr[i].wait_recv()
        v_row[i] = two_parts(couple(t_row[i]))

    parts = {}
    for j in range(1, nc):
        ec[j].wait_recv()
        right[j] = right_of(e_col[j])
        part_out[j] = make_and_apply(j)
        parts[j] = to_col(part_out.at[j], part_in.at[j], s_p, r_p, j)
        parts[j].start()
        sent.append(parts[j])
    own = apply(0)
    targets = t_row[0]
    for j in parts:
        parts[j].wait_recv()
        own = own + part_in[j]
    image = own + noise * targets

    def lanes(x):
        total = None
        for r in range(0, tasks, 8):
            for c in range(0, width, 128):
                piece = x[r : r + 8, c : c + 128]
                total = piece if total is None else total + piece
        return total

    cu_row[0, :tasks] = couple(image)
    cu_row[0, tasks:, :128] = lanes(targets * targets)
    cu_row[0, tasks:, 128:] = lanes(targets * image)
    cus = {}
    for k in range(1, nr):
        cus[k] = to_row(cu_row.at[0], cu_row.at[k], s_c, r_c, k)
        cus[k].start()
        sent.append(cus[k])
    v_row[0] = two_parts(cu_row[0, :tasks])
    sums = cu_row[0, tasks:]
    for k in range(1, nr):
        cus[k].wait_recv()
        v_row[k] = two_parts(cu_row[k, :tasks])
        sums = sums + cu_row[k, tasks:]

    mixes = {}
    for j in range(1, nc):
        mix_out[j, :tasks] = apply(j)
        mix_out[j, tasks:] = sums
        mixes[j] = to_col(mix_out.at[j], mix_in.at[j], s_m, r_m, j)
        mixes[j].start()
        sent.append(mixes[j])
    second = apply(0)
    for j in mixes:
        mixes[j].wait_recv()
        second = second + mix_in[j, :tasks]
        sums = sums + mix_in[j, tasks:]
    second = second + noise * image

    def total(x):
        return jnp.sum(jnp.sum(x, axis=1, keepdims=True), axis=0, keepdims=True)

    tt, tu = total(sums[:, :128]), total(sums[:, 128:])
    alpha = tt / tu
    residual = targets - alpha * image
    image_r = image - alpha * second

    rr, ra, ru = (total(lanes(residual * x)) for x in (residual, image_r, image))
    lane = lax.broadcasted_iota(jnp.int32, (1, 128), 1)
    mine = jnp.where(lane == 0, rr, jnp.where(lane == 1, ra, jnp.where(lane == 2, ru, 0.0)))
    scal[0] = mine
    finals = []
    for r in range(nr):
        for c in range(nc):
            k = r * nc + c
            if k:
                copy = pltpu.make_async_remote_copy(
                    src_ref=scal.at[0], dst_ref=scal.at[k], send_sem=s_s.at[k], recv_sem=r_s.at[k],
                    device_id={"row": rows_to[r][0], "col": cols_to[c][0]}, device_id_type=MESH)
                copy.start()
                finals.append((k, copy))
                sent.append(copy)
    for k, copy in finals:
        copy.wait_recv()
        mine = mine + scal[k]

    def pick(i):
        return jnp.sum(jnp.where(lane == i, mine, 0.0), axis=1, keepdims=True)

    rr, ra, ru = pick(0), pick(1), pick(2)
    beta = rr / tt
    direction = residual + beta * targets
    image_d = image_r + beta * image
    alpha2 = rr / (ra + 2.0 * beta * ru + beta * beta * tu)
    sol_ref[...] = alpha * targets + alpha2 * direction
    res_ref[...] = residual - alpha2 * image_d
    for copy in sent:
        copy.wait_send()


def solution(mesh):
    nr, nc = mesh.shape["row"], mesh.shape["col"]

    def on_device(embeddings, inv_length, task_cov, noise, targets):
        emb, width = embeddings.shape
        tasks = targets.shape[0]
        depth = -(-(6 * emb + 16) // 256) * 256
        dma = pltpu.SemaphoreType.DMA
        out = jax.ShapeDtypeStruct((tasks, width), F32)
        tiles = nr * nc * width * width
        return pl.pallas_call(
            functools.partial(kernel, nr, nc),
            out_shape=(out, out),
            in_specs=[pl.BlockSpec(memory_space=pl.ANY)] * 5,
            out_specs=(pl.BlockSpec(memory_space=pltpu.VMEM),) * 2,
            scratch_shapes=[
                pltpu.VMEM((1, emb), F32),
                pltpu.VMEM((tasks, tasks), F32),
                pltpu.VMEM((1, tasks), F32),
                pltpu.VMEM((nr, emb, width), F32),
                pltpu.VMEM((nc, emb, width), F32),
                pltpu.VMEM((nr, tasks, width), F32),
                pltpu.VMEM((tasks, tasks, 128), F32),
                pltpu.VMEM((nr, width, depth), BF16),
                pltpu.VMEM((nc, depth, width), BF16),
                pltpu.VMEM((nc, nr, width, width), BF16),
                pltpu.VMEM((nc, nr, width, width), BF16),
                pltpu.VMEM((nr, 2 * tasks, width), BF16),
                pltpu.VMEM((nc, tasks, width), F32),
                pltpu.VMEM((nc, tasks, width), F32),
                pltpu.VMEM((nr, tasks + 8, width), F32),
                pltpu.VMEM((nc, tasks + 8, width), F32),
                pltpu.VMEM((nc, tasks + 8, width), F32),
                pltpu.VMEM((nr * nc, 1, 128), F32),
                dma((5,)),
                dma((nr,)), dma((nr,)),
                dma((nc,)), dma((nc,)),
                dma((nr,)), dma((nr,)),
                dma((nc,)), dma((nc,)),
                dma((nr,)), dma((nr,)),
                dma((nc,)), dma((nc,)),
                dma((nr * nc,)), dma((nr * nc,)),
            ],
            compiler_params=pltpu.CompilerParams(
                collective_id=0, has_side_effects=True, vmem_limit_bytes=56 * 2**20
            ),
            cost_estimate=pl.CostEstimate(
                flops=2 * tiles * (depth + 8 * tasks), bytes_accessed=4 * width * (emb + 3 * tasks), transcendentals=tiles
            ),
        )(embeddings, inv_length.reshape(1, emb), task_cov, noise.reshape(1, tasks), targets)

    spread = P(None, ("groups", "row", "col"))
    return jax.shard_map(
        on_device,
        mesh=mesh,
        in_specs=(spread, P(), P(), P(), spread),
        out_specs=(spread, spread),
        check_vma=False,
    )
```

time: 220 us -> 30.4 us (0.14)
  blocking collectives: 196 us -> 0 us
  Pallas kernels: 0 us -> 27.6 us
  matrix products: 17 us -> 0 us
  between operations: 4.73 us -> 0.65 us
    all_gather x3 -> x0, blocking collectives: 102 us -> none  [the longest x2 63.5 us: on_device(): lax.all_gather(direction, ('row', 'col'), axis=1, tiled=True)]
    psum x3 -> x0, blocking collectives: 93.4 us -> none  [the longest x2 62.8 us: squares(): return lax.psum(jnp.sum(residual * residual), ('row', 'col'))]
    pallas_call x0 -> x1, Pallas kernels: none -> 27.6 us  [on_device(): pl.pallas_call(functools.partial(kernel, nr, nc), out_shape=(out, out), i...]
    dot_general x5 -> x0, matrix products: 17 us -> none  [the longest x2 10.6 us: on_device(): jnp.dot(lax.all_gather(direction, ('row', 'col'), axis=1, tiled=True), ti...]
where the time goes in v1:
time: 30.4 us; the launch traced here: 30.2 us
  Pallas kernels  27.6 us (91%)
  local copies, waits for them, and re-layouts  1.94 us (6%)
  between operations  0.65 us (2%)
    pallas_call x1, Pallas kernels, on_device(): pl.pallas_call(functools.partial(kernel, nr, nc), out_shape=(out, out), i...  27.6 us
    unnamed x4, local copies, waits for them, and re-layouts  1.94 us

profile of v1, /device:TPU:0, one launch (start us, length us, event | category | flops | bytes accessed | tf_op | source)
XLA Modules:
  0.0 30.2 jit_solution(821173722034539897)
XLA Ops:
  0.6 27.6 %shard_map.68 = (f32[16,256]{1,0:T(8,128)}, f32[16,256]{1,0:T(8,128)}) custom-call(f32[32,256]{1,0:T(8,128)} %e_hbm.1, f32[1,32]{1,0:T(1,128)} %bitcast.2, f32[16,16]{1,0:T(8,128)} %cov_hbm.1, f32[1,16]{1,0:T(1,128)} %bitcast.3, f32[16,256]{1,0:T(8,128)} %t_hbm.1), custom_call_target="tpu_custom_call" | custom-call | flops 805306368 | bytes 81920 | tf_op jit(solution)/shard_map/pallas_call | solution.py:291
  28.3 0.0 copy-start
  28.3 1.3 %copy.9 = f32[16,256]{1,0:T(8,128)} copy(f32[16,256]{1,0:T(8,128)} %get-tuple-element.4) | data formatting | bytes 32768
  29.6 0.0 copy-done
  29.6 0.6 %copy.10 = f32[16,256]{1,0:T(8,128)} copy(f32[16,256]{1,0:T(8,128)S(1)} %copy-done) | data formatting | bytes 32768
Async XLA Ops:
  28.3 1.3 %copy-start = (f32[16,256]{1,0:T(8,128)S(1)}, f32[16,256]{1,0:T(8,128)}, u32[]{:S(2)}) copy-start(f32[16,256]{1,0:T(8,128)} %get-tuple-element.5) | copy-start | bytes 49156

commit v2 on v1

--- a/solution.py
+++ b/solution.py
@@ -15,15 +15,13 @@
 
 
 def partner(me, k, n):
-    if n & (n - 1):
-        return [(me + k) % n, (me + n - k) % n][: 1 if 2 * k == n else 2]
-    other = me
+    assert n & (n - 1) == 0
     bit = 1
     while bit <= k:
         if k & bit:
-            other = other + bit * (1 - 2 * ((me // bit) % 2))
+            me = me + bit * (1 - 2 * ((me // bit) % 2))
         bit *= 2
-    return [other]
+    return me
 
 
 def three_parts(x):
@@ -39,10 +37,10 @@
     return jnp.concatenate([high, (x - high.astype(F32)).astype(BF16)], axis=0)
 
 
-def kernel(nr, nc, e_hbm, len_hbm, cov_hbm, noise_hbm, t_hbm, sol_ref, res_ref,
-           len_v, cov_v, noise_v, e_row, e_col, t_row, cov_b, left, right, k_high, k_low, v_row,
-           part_out, part_in, cu_row, mix_out, mix_in, scal,
-           sem_local, s_er, r_er, s_ec, r_ec, s_t, r_t, s_p, r_p, s_c, r_c, s_m, r_m, s_s, r_s):
+def kernel(nr, nc, e_hbm, len_hbm, cov_hbm, noise_hbm, t_hbm, out_ref,
+           len_v, cov_v, noise_v, e_row, e_col, t_row, t_col, cov_b, left, right, k_high, k_low, v_row,
+           acc_row, part_out, part_in, mix_out, mix_in, scal,
+           sem_local, s_er, r_er, s_ec, r_ec, s_t, r_t, s_u, r_u, s_p, r_p, s_m, r_m, s_s, r_s):
     emb, width = e_hbm.shape
     tasks = t_hbm.shape[0]
     row, col = lax.axis_index("row"), lax.axis_index("col")
@@ -51,12 +49,9 @@
 
     barrier = pltpu.get_barrier_semaphore()
     for k in range(1, nc):
-        for peer in cols_to[k]:
-            pl.semaphore_signal(barrier, inc=1, device_id={"col": peer}, device_id_type=MESH)
+        pl.semaphore_signal(barrier, inc=1, device_id={"col": cols_to[k]}, device_id_type=MESH)
     for k in range(1, nr):
-        for peer in rows_to[k]:
-            pl.semaphore_signal(barrier, inc=1, device_id={"row": peer}, device_id_type=MESH)
-    count = sum(len(p) for p in cols_to[1:] + rows_to[1:])
+        pl.semaphore_signal(barrier, inc=1, device_id={"row": rows_to[k]}, device_id_type=MESH)
 
     local = [
         pltpu.make_async_copy(src, dst, sem_local.at[i])
@@ -66,24 +61,25 @@
     ]
     for copy in local:
         copy.start()
-    pl.semaphore_wait(barrier, count)
+    pl.semaphore_wait(barrier, nc + nr - 2)
 
     def to_col(src, dst, send, recv, k):
         return pltpu.make_async_remote_copy(
             src_ref=src, dst_ref=dst, send_sem=send.at[k], recv_sem=recv.at[k],
-            device_id={"col": cols_to[k][0]}, device_id_type=MESH)
+            device_id={"col": cols_to[k]}, device_id_type=MESH)
 
     def to_row(src, dst, send, recv, k):
         return pltpu.make_async_remote_copy(
             src_ref=src, dst_ref=dst, send_sem=send.at[k], recv_sem=recv.at[k],
-            device_id={"row": rows_to[k][0]}, device_id_type=MESH)
+            device_id={"row": rows_to[k]}, device_id_type=MESH)
 
     sent = []
     ec = {k: to_col(e_hbm, e_col.at[k], s_ec, r_ec, k) for k in range(1, nc)}
     er = {k: to_row(e_hbm, e_row.at[k], s_er, r_er, k) for k in range(1, nr)}
     tr = {k: to_row(t_hbm, t_row.at[k], s_t, r_t, k) for k in range(1, nr)}
-    for group in (er, ec, tr):
-        for k in group:
+    tc = {k: to_col(t_hbm, t_col.at[k], s_u, r_u, k) for k in range(1, nc)}
+    for group in (ec, er, tc, tr):
+        for k in reversed(group):
             group[k].start()
             sent.append(group[k])
 
@@ -153,52 +149,53 @@
     def fold(acc):
         return acc[:tasks] + acc[tasks:]
 
-    def zero():
-        return jnp.zeros((2 * tasks, width), F32)
+    right[0] = right_of(e_row[0])
+    for i in range(nr):
+        if i:
+            er[i].wait_recv()
+        left[i] = left_of(e_row[i])
+    for j in range(nc):
+        if j:
+            ec[j].wait_recv()
+            right[j] = right_of(e_col[j])
+            tc[j].wait_recv()
+        v = two_parts(couple(t_col[j] if j else t_row[0]))
+
+        last = j + 1 == nc
+
+        def body(i, carry):
+            high, low = tile(j, i)
+            across = (((1,), (1,)), ((), ()))
+            acc = lax.dot_general(v, high, across, preferred_element_type=F32)
+            acc = acc + lax.dot_general(v, low, across, preferred_element_type=F32)
+            if j:
+                acc = acc + acc_row[i]
+            if last:
+                part_out[i] = fold(acc)
+            else:
+                acc_row[i] = acc
+            return carry
+        if not last:
+            over_rows(body, 0)
+
+    pieces = min(nr, 4)
+    each = nr // pieces
+    parts = []
+    for piece in range(pieces):
+        for i in range(piece * each, (piece + 1) * each):
+            body(i, 0)
+        here = pl.ds(piece * each, each)
+        for k in reversed(range(1, nr)):
+            parts.append(to_row(part_out.at[here], part_in.at[k, here], s_p.at[piece], r_p.at[piece], k))
+            parts[-1].start()
+    sent += parts
 
     def apply(j):
         def body(i, acc):
             v = v_row[i]
             acc = acc + jnp.dot(v, k_high[j, i], preferred_element_type=F32)
             return acc + jnp.dot(v, k_low[j, i], preferred_element_type=F32)
-        return fold(over_rows(body, zero()))
-
-    def make_and_apply(j):
-        def body(i, acc):
-            high, low = tile(j, i)
-            v = v_row[i]
-            acc = acc + jnp.dot(v, high, preferred_element_type=F32)
-            return acc + jnp.dot(v, low, preferred_element_type=F32)
-        return fold(over_rows(body, zero()))
-
-    right[0] = right_of(e_row[0])
-    for i in range(nr):
-        if i:
-            er[i].wait_recv()
-        left[i] = left_of(e_row[i])
-        if nr <= 4:
-            tile(0, i)
-    if nr > 4:
-        over_rows(lambda i, acc: (tile(0, i), acc)[1], 0)
-    for i in range(nr):
-        if i:
-            tr[i].wait_recv()
-        v_row[i] = two_parts(couple(t_row[i]))
-
-    parts = {}
-    for j in range(1, nc):
-        ec[j].wait_recv()
-        right[j] = right_of(e_col[j])
-        part_out[j] = make_and_apply(j)
-        parts[j] = to_col(part_out.at[j], part_in.at[j], s_p, r_p, j)
-        parts[j].start()
-        sent.append(parts[j])
-    own = apply(0)
-    targets = t_row[0]
-    for j in parts:
-        parts[j].wait_recv()
-        own = own + part_in[j]
-    image = own + noise * targets
+        return fold(over_rows(body, jnp.zeros((2 * tasks, width), F32)))
 
     def lanes(x):
         total = None
@@ -208,25 +205,29 @@
                 total = piece if total is None else total + piece
         return total
 
-    cu_row[0, :tasks] = couple(image)
-    cu_row[0, tasks:, :128] = lanes(targets * targets)
-    cu_row[0, tasks:, 128:] = lanes(targets * image)
-    cus = {}
+    targets = t_row[0]
     for k in range(1, nr):
-        cus[k] = to_row(cu_row.at[0], cu_row.at[k], s_c, r_c, k)
-        cus[k].start()
-        sent.append(cus[k])
-    v_row[0] = two_parts(cu_row[0, :tasks])
-    sums = cu_row[0, tasks:]
-    for k in range(1, nr):
-        cus[k].wait_recv()
-        v_row[k] = two_parts(cu_row[k, :tasks])
-        sums = sums + cu_row[k, tasks:]
+        tr[k].wait_recv()
+    for copy in parts:
+        copy.wait_recv()
+    tt = tu = None
+    for i in range(nr):
+        field = part_out[i]
+        for k in range(1, nr):
+            field = field + part_in[k, i ^ k]
+        field = field + noise * t_row[i]
+        if i == 0:
+            image = field
+        v_row[i] = two_parts(field)
+        more_tt, more_tu = lanes(t_row[i] * t_row[i]), lanes(t_row[i] * field)
+        tt = more_tt if tt is None else tt + more_tt
+        tu = more_tu if tu is None else tu + more_tu
+    sums = jnp.concatenate([tt, tu], axis=1)
 
     mixes = {}
-    for j in range(1, nc):
+    for j in reversed(range(1, nc)):
         mix_out[j, :tasks] = apply(j)
-        mix_out[j, tasks:] = sums
+        mix_out[j, tasks:, :256] = sums
         mixes[j] = to_col(mix_out.at[j], mix_in.at[j], s_m, r_m, j)
         mixes[j].start()
         sent.append(mixes[j])
@@ -234,8 +235,8 @@
     for j in mixes:
         mixes[j].wait_recv()
         second = second + mix_in[j, :tasks]
-        sums = sums + mix_in[j, tasks:]
-    second = second + noise * image
+        sums = sums + mix_in[j, tasks:, :256]
+    second = couple(second) + noise * image
 
     def total(x):
         return jnp.sum(jnp.sum(x, axis=1, keepdims=True), axis=0, keepdims=True)
@@ -250,13 +251,13 @@
     mine = jnp.where(lane == 0, rr, jnp.where(lane == 1, ra, jnp.where(lane == 2, ru, 0.0)))
     scal[0] = mine
     finals = []
-    for r in range(nr):
-        for c in range(nc):
+    for r in reversed(range(nr)):
+        for c in reversed(range(nc)):
             k = r * nc + c
             if k:
                 copy = pltpu.make_async_remote_copy(
                     src_ref=scal.at[0], dst_ref=scal.at[k], send_sem=s_s.at[k], recv_sem=r_s.at[k],
-                    device_id={"row": rows_to[r][0], "col": cols_to[c][0]}, device_id_type=MESH)
+                    device_id={"row": rows_to[r], "col": cols_to[c]}, device_id_type=MESH)
                 copy.start()
                 finals.append((k, copy))
                 sent.append(copy)
@@ -272,8 +273,8 @@
     direction = residual + beta * targets
     image_d = image_r + beta * image
     alpha2 = rr / (ra + 2.0 * beta * ru + beta * beta * tu)
-    sol_ref[...] = alpha * targets + alpha2 * direction
-    res_ref[...] = residual - alpha2 * image_d
+    out_ref[: tasks] = alpha * targets + alpha2 * direction
+    out_ref[tasks :] = residual - alpha2 * image_d
     for copy in sent:
         copy.wait_send()
 
@@ -288,11 +289,11 @@
         dma = pltpu.SemaphoreType.DMA
         out = jax.ShapeDtypeStruct((tasks, width), F32)
         tiles = nr * nc * width * width
-        return pl.pallas_call(
+        both = pl.pallas_call(
             functools.partial(kernel, nr, nc),
-            out_shape=(out, out),
+            out_shape=pltpu.VMEM((2 * tasks, width), F32),
             in_specs=[pl.BlockSpec(memory_space=pl.ANY)] * 5,
-            out_specs=(pl.BlockSpec(memory_space=pltpu.VMEM),) * 2,
+            out_specs=pl.BlockSpec(memory_space=pltpu.VMEM),
             scratch_shapes=[
                 pltpu.VMEM((1, emb), F32),
                 pltpu.VMEM((tasks, tasks), F32),
@@ -300,15 +301,16 @@
                 pltpu.VMEM((nr, emb, width), F32),
                 pltpu.VMEM((nc, emb, width), F32),
                 pltpu.VMEM((nr, tasks, width), F32),
+                pltpu.VMEM((nc, tasks, width), F32),
                 pltpu.VMEM((tasks, tasks, 128), F32),
                 pltpu.VMEM((nr, width, depth), BF16),
                 pltpu.VMEM((nc, depth, width), BF16),
                 pltpu.VMEM((nc, nr, width, width), BF16),
                 pltpu.VMEM((nc, nr, width, width), BF16),
                 pltpu.VMEM((nr, 2 * tasks, width), BF16),
-                pltpu.VMEM((nc, tasks, width), F32),
-                pltpu.VMEM((nc, tasks, width), F32),
-                pltpu.VMEM((nr, tasks + 8, width), F32),
+                pltpu.VMEM((nr, 2 * tasks, width), F32),
+                pltpu.VMEM((nr, tasks, width), F32),
+                pltpu.VMEM((nr, nr, tasks, width), F32),
                 pltpu.VMEM((nc, tasks + 8, width), F32),
                 pltpu.VMEM((nc, tasks + 8, width), F32),
                 pltpu.VMEM((nr * nc, 1, 128), F32),
@@ -317,7 +319,7 @@
                 dma((nc,)), dma((nc,)),
                 dma((nr,)), dma((nr,)),
                 dma((nc,)), dma((nc,)),
-                dma((nr,)), dma((nr,)),
+                dma((min(nr, 4), nr)), dma((min(nr, 4), nr)),
                 dma((nc,)), dma((nc,)),
                 dma((nr * nc,)), dma((nr * nc,)),
             ],
@@ -328,6 +330,7 @@
                 flops=2 * tiles * (depth + 8 * tasks), bytes_accessed=4 * width * (emb + 3 * tasks), transcendentals=tiles
             ),
         )(embeddings, inv_length.reshape(1, emb), task_cov, noise.reshape(1, tasks), targets)
+        return both[:tasks], both[tasks:]
 
     spread = P(None, ("groups", "row", "col"))
     return jax.shard_map(

time: 30.4 us -> 27.3 us (0.90)
  Pallas kernels: 27.6 us -> 25.9 us
  local copies, waits for them, and re-layouts: 1.94 us -> 0.61 us
    unnamed x4 -> x0, local copies, waits for them, and re-layouts: 1.94 us -> none
    pallas_call x1, Pallas kernels: 27.6 us -> 25.9 us  [on_device(): pl.pallas_call(functools.partial(kernel, nr, nc), out_shape=pltpu.VMEM((2...]
    slice x0 -> x1, local copies, waits for them, and re-layouts: none -> 0.61 us  [on_device(): return (both[:tasks], both[tasks:])]
where the time goes in v2:
time: 27.3 us; the launch traced here: 27.2 us
  Pallas kernels  25.9 us (95%)
  between operations  0.64 us (2%)
  local copies, waits for them, and re-layouts  0.61 us (2%)
    pallas_call x1, Pallas kernels, on_device(): pl.pallas_call(functools.partial(kernel, nr, nc), out_shape=pltpu.VMEM((2...  25.9 us
    slice x1, local copies, waits for them, and re-layouts, on_device(): return (both[:tasks], both[tasks:])  0.61 us

profile of v2, /device:TPU:0, one launch (start us, length us, event | category | flops | bytes accessed | tf_op | source)
XLA Modules:
  0.0 27.2 jit_solution(12805756491457958904)
XLA Ops:
  0.6 25.9 %shard_map.68 = f32[32,256]{1,0:T(8,128)S(1)} custom-call(f32[32,256]{1,0:T(8,128)} %e_hbm.1, f32[1,32]{1,0:T(1,128)} %bitcast.2, f32[16,16]{1,0:T(8,128)} %cov_hbm.1, f32[1,16]{1,0:T(1,128)} %bitcast.3, f32[16,256]{1,0:T(8,128)} %t_hbm.1), custom_call_target="tpu_custom_call" | custom-call | flops 805306368 | bytes 81920 | tf_op jit(solution)/shard_map/pallas_call | solution.py:292
  26.6 0.6 %fusion = (f32[16,256]{1,0:T(8,128)}, f32[16,256]{1,0:T(8,128)}) fusion(f32[32,256]{1,0:T(8,128)S(1)} %shard_map.68), kind=kLoop, calls=%fused_computation | loop fusion | bytes 65536 | tf_op jit(solution)/shard_map/slice | solution.py:333

commit v3 on v2

--- a/solution.py
+++ b/solution.py
@@ -39,8 +39,8 @@
 
 def kernel(nr, nc, e_hbm, len_hbm, cov_hbm, noise_hbm, t_hbm, out_ref,
            len_v, cov_v, noise_v, e_row, e_col, t_row, t_col, cov_b, left, right, k_high, k_low, v_row,
-           acc_row, part_out, part_in, mix_out, mix_in, scal,
-           sem_local, s_er, r_er, s_ec, r_ec, s_t, r_t, s_u, r_u, s_p, r_p, s_m, r_m, s_s, r_s):
+           acc_row, row_out, row_in, col_out, col_in, mix_out, mix_in, scal,
+           sem_local, s_er, r_er, s_ec, r_ec, s_t, r_t, s_u, r_u, s_p, r_p, s_q, r_q, s_m, r_m, s_s, r_s):
     emb, width = e_hbm.shape
     tasks = t_hbm.shape[0]
     row, col = lax.axis_index("row"), lax.axis_index("col")
@@ -154,48 +154,52 @@
         if i:
             er[i].wait_recv()
         left[i] = left_of(e_row[i])
+    for i in range(nr):
+        if i:
+            tr[i].wait_recv()
+        v_row[i] = two_parts(couple(t_row[i]))
+    pieces = min(nr, 4)
+    each = nr // pieces
+    row_sums, col_sums = [], []
     for j in range(nc):
         if j:
             ec[j].wait_recv()
             right[j] = right_of(e_col[j])
             tc[j].wait_recv()
-        v = two_parts(couple(t_col[j] if j else t_row[0]))
-
+        v_col = two_parts(couple(t_col[j])) if j else v_row[0]
         last = j + 1 == nc
 
-        def body(i, carry):
+        def body(i, acc):
             high, low = tile(j, i)
             across = (((1,), (1,)), ((), ()))
-            acc = lax.dot_general(v, high, across, preferred_element_type=F32)
-            acc = acc + lax.dot_general(v, low, across, preferred_element_type=F32)
+            total = lax.dot_general(v_col, high, across, preferred_element_type=F32)
+            total = total + lax.dot_general(v_col, low, across, preferred_element_type=F32)
             if j:
-                acc = acc + acc_row[i]
+                total = total + acc_row[i]
             if last:
-                part_out[i] = fold(acc)
+                row_out[i] = fold(total)
             else:
-                acc_row[i] = acc
-            return carry
+                acc_row[i] = total
+            v = v_row[i]
+            acc = acc + jnp.dot(v, high, preferred_element_type=F32)
+            return acc + jnp.dot(v, low, preferred_element_type=F32)
+
+        acc = jnp.zeros((2 * tasks, width), F32)
         if not last:
-            over_rows(body, 0)
-
-    pieces = min(nr, 4)
-    each = nr // pieces
-    parts = []
-    for piece in range(pieces):
-        for i in range(piece * each, (piece + 1) * each):
-            body(i, 0)
-        here = pl.ds(piece * each, each)
-        for k in reversed(range(1, nr)):
-            parts.append(to_row(part_out.at[here], part_in.at[k, here], s_p.at[piece], r_p.at[piece], k))
-            parts[-1].start()
-    sent += parts
-
-    def apply(j):
-        def body(i, acc):
-            v = v_row[i]
-            acc = acc + jnp.dot(v, k_high[j, i], preferred_element_type=F32)
-            return acc + jnp.dot(v, k_low[j, i], preferred_element_type=F32)
-        return fold(over_rows(body, jnp.zeros((2 * tasks, width), F32)))
+            acc = over_rows(body, acc)
+        else:
+            for piece in range(pieces):
+                for i in range(piece * each, (piece + 1) * each):
+                    acc = body(i, acc)
+                here = pl.ds(piece * each, each)
+                for k in reversed(range(1, nr)):
+                    row_sums.append(to_row(row_out.at[here], row_in.at[k, here], s_p.at[piece], r_p.at[piece], k))
+                    row_sums[-1].start()
+        col_out[j] = fold(acc)
+        for k in reversed(range(1, nc)):
+            col_sums.append(to_col(col_out.at[j], col_in.at[k, j], s_q.at[j], r_q.at[j], k))
+            col_sums[-1].start()
+    sent += row_sums + col_sums
 
     def lanes(x):
         total = None
@@ -205,50 +209,61 @@
                 total = piece if total is None else total + piece
         return total
 
-    targets = t_row[0]
-    for k in range(1, nr):
-        tr[k].wait_recv()
-    for copy in parts:
-        copy.wait_recv()
-    tt = tu = None
-    for i in range(nr):
-        field = part_out[i]
-        for k in range(1, nr):
-            field = field + part_in[k, i ^ k]
-        field = field + noise * t_row[i]
-        if i == 0:
-            image = field
-        v_row[i] = two_parts(field)
-        more_tt, more_tu = lanes(t_row[i] * t_row[i]), lanes(t_row[i] * field)
-        tt = more_tt if tt is None else tt + more_tt
-        tu = more_tu if tu is None else tu + more_tu
-    sums = jnp.concatenate([tt, tu], axis=1)
-
-    mixes = {}
-    for j in reversed(range(1, nc)):
-        mix_out[j, :tasks] = apply(j)
-        mix_out[j, tasks:, :256] = sums
-        mixes[j] = to_col(mix_out.at[j], mix_in.at[j], s_m, r_m, j)
-        mixes[j].start()
-        sent.append(mixes[j])
-    second = apply(0)
-    for j in mixes:
-        mixes[j].wait_recv()
-        second = second + mix_in[j, :tasks]
-        sums = sums + mix_in[j, tasks:, :256]
-    second = couple(second) + noise * image
-
     def total(x):
         return jnp.sum(jnp.sum(x, axis=1, keepdims=True), axis=0, keepdims=True)
 
-    tt, tu = total(sums[:, :128]), total(sums[:, 128:])
-    alpha = tt / tu
-    residual = targets - alpha * image
-    image_r = image - alpha * second
-
-    rr, ra, ru = (total(lanes(residual * x)) for x in (residual, image_r, image))
+    def added(terms):
+        return functools.reduce(lambda a, b: a + b, terms)
+
+    for copy in row_sums:
+        copy.wait_recv()
+    images = []
+    for i in range(nr):
+        field = added([row_out[i]] + [row_in[k, i ^ k] for k in range(1, nr)]) + noise * t_row[i]
+        v_row[i] = two_parts(field)
+        images.append(field)
+
+    def apply(j):
+        def body(i, acc):
+            v = v_row[i]
+            acc = acc + jnp.dot(v, k_high[j, i], preferred_element_type=F32)
+            return acc + jnp.dot(v, k_low[j, i], preferred_element_type=F32)
+        return couple(fold(over_rows(body, jnp.zeros((2 * tasks, width), F32))))
+
+    mixes = {}
+    for j in reversed(range(nc)):
+        mix_out[j] = apply(j)
+        if j:
+            mixes[j] = to_col(mix_out.at[j], mix_in.at[j], s_m, r_m, j)
+            mixes[j].start()
+            sent.append(mixes[j])
+
+    targets, image = t_row[0], images[0]
+    tt = total(added([lanes(t_row[i] * t_row[i]) for i in range(nr)]))
+    tu = total(added([lanes(t_row[i] * images[i]) for i in range(nr)]))
+    about = tt / tu
+    near = [t_row[i] - about * images[i] for i in range(nr)]
+    rr = total(added([lanes(x * x) for x in near]))
+    ru = total(added([lanes(x * u) for x, u in zip(near, images)]))
+    uu = total(added([lanes(u * u) for u in images]))
+
+    for copy in col_sums:
+        copy.wait_recv()
+    xx, xu, ww = [noise * near[0] * near[0]], [2.0 * noise * near[0] * image], [noise * image * image]
+    for j in range(nc):
+        goal = t_col[j] if j else targets
+        field = added([col_out[j]] + [col_in[k, j ^ k] for k in range(1, nc)]) + noise * goal
+        x = goal - about * field
+        of_u = mix_out[j]
+        of_x = col_out[j] - about * of_u
+        xx.append(x * of_x)
+        xu.append(field * of_x + x * of_u)
+        ww.append(field * of_u)
     lane = lax.broadcasted_iota(jnp.int32, (1, 128), 1)
-    mine = jnp.where(lane == 0, rr, jnp.where(lane == 1, ra, jnp.where(lane == 2, ru, 0.0)))
+    mine = jnp.zeros((1, 128), F32)
+    values = [total(lanes(added(terms))) for terms in (xx, xu, ww)] + [about, tt, tu, rr, ru, uu]
+    for place, value in enumerate(values):
+        mine = jnp.where(lane == place, value, mine)
     scal[0] = mine
     finals = []
     for r in reversed(range(nr)):
@@ -261,14 +276,37 @@
                 copy.start()
                 finals.append((k, copy))
                 sent.append(copy)
+
+    second = mix_out[0] + noise * image
+    for j in mixes:
+        mixes[j].wait_recv()
+        second = second + mix_in[j]
+
+    count = nr * nc
+    place = lax.broadcasted_iota(jnp.int32, (count, 128), 0)
+    table = jnp.broadcast_to(mine, (count, 128))
     for k, copy in finals:
         copy.wait_recv()
-        mine = mine + scal[k]
-
-    def pick(i):
-        return jnp.sum(jnp.where(lane == i, mine, 0.0), axis=1, keepdims=True)
-
-    rr, ra, ru = pick(0), pick(1), pick(2)
+        table = jnp.where(place == k, jnp.broadcast_to(scal[k], (count, 128)), table)
+    lane = lax.broadcasted_iota(jnp.int32, (count, 128), 1)
+
+    tt = total(jnp.where(lane == 4, table, 0.0)) * (1.0 / nr)
+    tu = total(jnp.where(lane == 5, table, 0.0)) * (1.0 / nr)
+    alpha = tt / tu
+    shift = alpha - jnp.sum(jnp.where(lane == 3, table, 0.0), axis=1, keepdims=True)
+
+    def moved(first, weights):
+        factor = jnp.zeros((count, 128), F32)
+        for i, weight in enumerate(weights):
+            factor = jnp.where(lane == first + i, weight, factor)
+        return total(factor * table)
+
+    ra = moved(0, [jnp.ones_like(shift), -shift, shift * shift])
+    rr = moved(6, [jnp.ones_like(shift), -2.0 * shift, shift * shift]) * (1.0 / nr)
+    ru = moved(7, [jnp.ones_like(shift), -shift]) * (1.0 / nr)
+
+    residual = targets - alpha * image
+    image_r = image - alpha * second
     beta = rr / tt
     direction = residual + beta * targets
     image_d = image_r + beta * image
@@ -311,8 +349,10 @@
                 pltpu.VMEM((nr, 2 * tasks, width), F32),
                 pltpu.VMEM((nr, tasks, width), F32),
                 pltpu.VMEM((nr, nr, tasks, width), F32),
-                pltpu.VMEM((nc, tasks + 8, width), F32),
-                pltpu.VMEM((nc, tasks + 8, width), F32),
+                pltpu.VMEM((nc, tasks, width), F32),
+                pltpu.VMEM((nc, nc, tasks, width), F32),
+                pltpu.VMEM((nc, tasks, width), F32),
+                pltpu.VMEM((nc, tasks, width), F32),
                 pltpu.VMEM((nr * nc, 1, 128), F32),
                 dma((5,)),
                 dma((nr,)), dma((nr,)),
@@ -320,6 +360,7 @@
                 dma((nr,)), dma((nr,)),
                 dma((nc,)), dma((nc,)),
                 dma((min(nr, 4), nr)), dma((min(nr, 4), nr)),
+                dma((nc, nc)), dma((nc, nc)),
                 dma((nc,)), dma((nc,)),
                 dma((nr * nc,)), dma((nr * nc,)),
             ],

time: 27.3 us -> 25.6 us (0.938)
  Pallas kernels: 25.9 us -> 24.2 us
    pallas_call x1, Pallas kernels: 25.9 us -> 24.2 us  [on_device(): pl.pallas_call(functools.partial(kernel, nr, nc), out_shape=pltpu.VMEM((2...]
where the time goes in v3:
time: 25.6 us; the launch traced here: 25.4 us
  Pallas kernels  24.2 us (95%)
  between operations  0.64 us (2%)
  local copies, waits for them, and re-layouts  0.61 us (2%)
    pallas_call x1, Pallas kernels, on_device(): pl.pallas_call(functools.partial(kernel, nr, nc), out_shape=pltpu.VMEM((2...  24.2 us
    slice x1, local copies, waits for them, and re-layouts, on_device(): return (both[:tasks], both[tasks:])  0.61 us

profile of v3, /device:TPU:0, one launch (start us, length us, event | category | flops | bytes accessed | tf_op | source)
XLA Modules:
  0.0 25.4 jit_solution(15015692973252829079)
XLA Ops:
  0.6 24.2 %shard_map.68 = f32[32,256]{1,0:T(8,128)S(1)} custom-call(f32[32,256]{1,0:T(8,128)} %e_hbm.1, f32[1,32]{1,0:T(1,128)} %bitcast.2, f32[16,16]{1,0:T(8,128)} %cov_hbm.1, f32[1,16]{1,0:T(1,128)} %bitcast.3, f32[16,256]{1,0:T(8,128)} %t_hbm.1), custom_call_target="tpu_custom_call" | custom-call | flops 805306368 | bytes 81920 | tf_op jit(solution)/shard_map/pallas_call | solution.py:330
  24.8 0.6 %fusion = (f32[16,256]{1,0:T(8,128)}, f32[16,256]{1,0:T(8,128)}) fusion(f32[32,256]{1,0:T(8,128)S(1)} %shard_map.68), kind=kLoop, calls=%fused_computation | loop fusion | bytes 65536 | tf_op jit(solution)/shard_map/slice | solution.py:374

commit v4 on v3

--- a/solution.py
+++ b/solution.py
@@ -73,17 +73,19 @@
             src_ref=src, dst_ref=dst, send_sem=send.at[k], recv_sem=recv.at[k],
             device_id={"row": rows_to[k]}, device_id_type=MESH)
 
+    for copy in local[:2]:
+        copy.wait()
     sent = []
-    ec = {k: to_col(e_hbm, e_col.at[k], s_ec, r_ec, k) for k in range(1, nc)}
-    er = {k: to_row(e_hbm, e_row.at[k], s_er, r_er, k) for k in range(1, nr)}
-    tr = {k: to_row(t_hbm, t_row.at[k], s_t, r_t, k) for k in range(1, nr)}
-    tc = {k: to_col(t_hbm, t_col.at[k], s_u, r_u, k) for k in range(1, nc)}
+    ec = {k: to_col(e_row.at[0], e_col.at[k], s_ec, r_ec, k) for k in range(1, nc)}
+    er = {k: to_row(e_row.at[0], e_row.at[k], s_er, r_er, k) for k in range(1, nr)}
+    tr = {k: to_row(t_row.at[0], t_row.at[k], s_t, r_t, k) for k in range(1, nr)}
+    tc = {k: to_col(t_row.at[0], t_col.at[k], s_u, r_u, k) for k in range(1, nc)}
     for group in (ec, er, tc, tr):
         for k in reversed(group):
             group[k].start()
             sent.append(group[k])
 
-    for copy in local:
+    for copy in local[2:]:
         copy.wait()
 
     def as_column(x, n):
@@ -165,40 +167,44 @@
         if j:
             ec[j].wait_recv()
             right[j] = right_of(e_col[j])
+        last = j + 1 == nc
+
+        def ahead(i, acc):
+            high, low = tile(j, i)
+            v = v_row[i]
+            acc = acc + jnp.dot(v, high, preferred_element_type=F32)
+            return acc + jnp.dot(v, low, preferred_element_type=F32)
+
+        col_out[j] = fold(over_rows(ahead, jnp.zeros((2 * tasks, width), F32)))
+        for k in reversed(range(1, nc)):
+            col_sums.append(to_col(col_out.at[j], col_in.at[k, j], s_q.at[j], r_q.at[j], k))
+            col_sums[-1].start()
+        if j:
             tc[j].wait_recv()
         v_col = two_parts(couple(t_col[j])) if j else v_row[0]
-        last = j + 1 == nc
-
-        def body(i, acc):
-            high, low = tile(j, i)
-            across = (((1,), (1,)), ((), ()))
-            total = lax.dot_general(v_col, high, across, preferred_element_type=F32)
-            total = total + lax.dot_general(v_col, low, across, preferred_element_type=F32)
+
+        def across(i, carry):
+            both = (((1,), (1,)), ((), ()))
+            total = lax.dot_general(v_col, k_high[j, i], both, preferred_element_type=F32)
+            total = total + lax.dot_general(v_col, k_low[j, i], both, preferred_element_type=F32)
             if j:
                 total = total + acc_row[i]
             if last:
                 row_out[i] = fold(total)
             else:
                 acc_row[i] = total
-            v = v_row[i]
-            acc = acc + jnp.dot(v, high, preferred_element_type=F32)
-            return acc + jnp.dot(v, low, preferred_element_type=F32)
-
-        acc = jnp.zeros((2 * tasks, width), F32)
+            return carry
+
         if not last:
-            acc = over_rows(body, acc)
-        else:
-            for piece in range(pieces):
-                for i in range(piece * each, (piece + 1) * each):
-                    acc = body(i, acc)
-                here = pl.ds(piece * each, each)
-                for k in reversed(range(1, nr)):
-                    row_sums.append(to_row(row_out.at[here], row_in.at[k, here], s_p.at[piece], r_p.at[piece], k))
-                    row_sums[-1].start()
-        col_out[j] = fold(acc)
-        for k in reversed(range(1, nc)):
-            col_sums.append(to_col(col_out.at[j], col_in.at[k, j], s_q.at[j], r_q.at[j], k))
-            col_sums[-1].start()
+            over_rows(across, 0)
+            continue
+        for piece in range(pieces):
+            for i in range(piece * each, (piece + 1) * each):
+                across(i, 0)
+            here = pl.ds(piece * each, each)
+            for k in reversed(range(1, nr)):
+                row_sums.append(to_row(row_out.at[here], row_in.at[k, here], s_p.at[piece], r_p.at[piece], k))
+                row_sums[-1].start()
     sent += row_sums + col_sums
 
     def lanes(x):

time: 25.6 us -> 24.6 us (0.961)
  Pallas kernels: 24.2 us -> 23.2 us
    pallas_call x1, Pallas kernels: 24.2 us -> 23.2 us  [on_device(): pl.pallas_call(functools.partial(kernel, nr, nc), out_shape=pltpu.VMEM((2...]
where the time goes in v4:
time: 24.6 us; the launch traced here: 24.5 us
  Pallas kernels  23.2 us (94%)
  between operations  0.64 us (3%)
  local copies, waits for them, and re-layouts  0.61 us (2%)
    pallas_call x1, Pallas kernels, on_device(): pl.pallas_call(functools.partial(kernel, nr, nc), out_shape=pltpu.VMEM((2...  23.2 us
    slice x1, local copies, waits for them, and re-layouts, on_device(): return (both[:tasks], both[tasks:])  0.61 us

profile of v4, /device:TPU:0, one launch (start us, length us, event | category | flops | bytes accessed | tf_op | source)
XLA Modules:
  0.0 24.5 jit_solution(1662768905825943773)
XLA Ops:
  0.6 23.2 %shard_map.68 = f32[32,256]{1,0:T(8,128)S(1)} custom-call(f32[32,256]{1,0:T(8,128)} %e_hbm.1, f32[1,32]{1,0:T(1,128)} %bitcast.2, f32[16,16]{1,0:T(8,128)} %cov_hbm.1, f32[1,16]{1,0:T(1,128)} %bitcast.3, f32[16,256]{1,0:T(8,128)} %t_hbm.1), custom_call_target="tpu_custom_call" | custom-call | flops 805306368 | bytes 81920 | tf_op jit(solution)/shard_map/pallas_call | solution.py:336
  23.9 0.6 %fusion = (f32[16,256]{1,0:T(8,128)}, f32[16,256]{1,0:T(8,128)}) fusion(f32[32,256]{1,0:T(8,128)S(1)} %shard_map.68), kind=kLoop, calls=%fused_computation | loop fusion | bytes 65536 | tf_op jit(solution)/shard_map/slice | solution.py:380
